TPU v7x, 512 devices: a whole 4x8x8 slice. The times are simulated.
512 devices in a mesh: grp: 16 (over y, core), blk: 32 (over z, x).
Axes of the slice: x: 4, y: 8, z: 8, core: 2. Of those that a mesh axis runs over, the one named last changes fastest.
Arguments:
- embeddings: float32 [65536, 1024], P(('grp', 'blk'))
- cluster_ids: int32 [65536], P(('grp', 'blk')), may hold values from 0 to 15, as said below
- row_slots: int32 [65536], P(('grp', 'blk')), may hold values from 0 to 15, as said below
- cluster_sizes: int32 [512, 16], P(('grp', 'blk')), may hold values from 0 to 16, as said below
Outputs:
- max_similarity: float32 [65536], P(('grp', 'blk'))
Inputs may be any that keep to these rules, and one draw needn't show every extreme that they name: `cluster_ids`: every cluster id is used; every cluster holds many rows. `row_slots`: the rows that one device owns of one cluster have the slots 0 to that count minus 1, each once. `cluster_sizes`: entry [d, c] is the number of rows of cluster c owned by device d (the device at index d of grp+blk); each row of it sums to 128.
All inputs are finite; a program needn't handle non-finite values.
Results may differ from a plain program's by a relative error of at most 0.0003.
Values may be sent and summed in bfloat16 or wider, within the bound.
A program may use at most 64 MiB of HBM per device.

v0:
```python
import jax
import jax.numpy as jnp
from jax import lax
from jax.sharding import PartitionSpec as P


def normalize_rows(embeddings):
    total = jnp.sum(embeddings * embeddings, axis=1, keepdims=True)
    return (embeddings * lax.rsqrt(total + 1e-06)).astype(jnp.bfloat16)


def pair_scores(left, right):
    return jnp.einsum("id,jd->ij", left, right, preferred_element_type=jnp.float32)


def body(embeddings, cluster_ids, row_slots, cluster_sizes):
    clusters = cluster_sizes.shape[1]
    feature_dim = embeddings.shape[1]
    owned_rows = embeddings.shape[0]
    slot_count = 2 * owned_rows // clusters
    unit_rows = normalize_rows(embeddings)
    outgoing = (
        jnp.zeros((clusters, slot_count, feature_dim), jnp.bfloat16)
        .at[cluster_ids, row_slots]
        .set(unit_rows)
    )
    counts = cluster_sizes.reshape(clusters, 1).astype(jnp.bfloat16)
    arrived, arrived_counts = (
        lax.all_to_all(outgoing, "grp", split_axis=0, concat_axis=0, tiled=True),
        lax.all_to_all(counts, "grp", split_axis=0, concat_axis=0, tiled=True),
    )
    block_rows = clusters * slot_count
    members = arrived.reshape(block_rows, feature_dim)
    slot_index = jnp.arange(slot_count, dtype=jnp.int32)
    alive_slot = (slot_index[None, :] < arrived_counts.astype(jnp.int32)).reshape(block_rows)
    alive_marker = alive_slot.astype(jnp.bfloat16)
    position = lax.axis_index("blk")
    row_index = jnp.arange(block_rows, dtype=jnp.int32)
    own_global = position * block_rows + row_index
    start_score = jnp.full((block_rows,), -4.0, jnp.float32)
    others = lax.all_gather(members, "blk", axis=0, tiled=True)
    marker = lax.all_gather(alive_marker, "blk", axis=0, tiled=True)
    scores = pair_scores(members, others)
    columns = jnp.arange(others.shape[0], dtype=jnp.int32)
    usable = (marker[None, :] > 0) & (own_global[:, None] != columns[None, :])
    top_score = jnp.maximum(start_score, jnp.max(jnp.where(usable, scores, -4.0), axis=1))
    owner_maxima = lax.all_to_all(
        top_score.reshape(clusters, slot_count), "grp", split_axis=0, concat_axis=0, tiled=True
    )
    return owner_maxima[cluster_ids, row_slots]


def solution(mesh):
    placed = (
        P(("grp", "blk"), None),
        P(("grp", "blk")),
        P(("grp", "blk")),
        P(("grp", "blk"), None),
    )
    return jax.shard_map(
        body, mesh=mesh, in_specs=placed, out_specs=P(("grp", "blk")), check_vma=False
    )
```

profile of v0, /device:TPU:1, one launch (start us, length us, event | category | flops | bytes accessed | tf_op | source)
XLA Modules:
  0.0 225.4 jit_solution(9092586551439022312)
XLA Ops:
  6.5 0.0 all-gather.3.cloned.1.call-start
  6.5 1.2 multiply_reduce_fusion
  7.7 1.1 multiply_convert_fusion
  8.9 0.7 fusion.7
  9.5 0.1 broadcast_in_dim.12
  9.6 8.9 %scatter_fusion = bf16[16,16,1024]{2,1,0:T(8,128)(2,1)S(1)} fusion(bf16[16,16,1024]{2,1,0:T(8,128)(2,1)S(1)} %broadcast_in_dim.12, s32[128]{0:T(128)S(1)} %get-tuple-element.6, bf16[128,1024]{1,0:T(8,128)(2,1)S(1)} %multiply_convert_fusion), kind=kCustom, calls=%fused_computation.1 | custom fusion | bytes 787456 | tf_op jit(solution)/shard_map/scatter | solution.py:25
  18.5 27.3 %all_to_all.20 = bf16[16,16,1024]{2,1,0:T(8,128)(2,1)} all-to-all(bf16[16,16,1024]{2,1,0:T(8,128)(2,1)S(1)} %scatter_fusion), channel_id=1, replica_groups=mesh['grp'=16,'blk'=32] {'grp'}, dimensions={0} | all-to-all | bytes 1048576 | tf_op jit(solution)/shard_map/all_to_all | solution.py:29
  45.9 0.0 all-gather.3.cloned.1.call-update
  45.9 0.7 convert_bitcast_fusion
  46.6 0.7 copy.6
  47.2 3.3 %all-to-all-start = ((bf16[16,1,1]{2,1,0:T(2,128)(2,1)}), bf16[16,1,1]{2,1,0:T(2,128)(2,1)S(1)}, u32[]{:S(2)}, u32[]{:S(2)}) async-start(bf16[16,1,1]{2,1,0:T(2,128)(2,1)} %copy.6), calls=%async_computation | async-start | bytes 16384 | tf_op jit(solution)/shard_map/all_to_all | solution.py:30
  50.6 6.6 %all-to-all-done = bf16[16,1,1]{2,1,0:T(2,128)(2,1)S(1)} async-done(((bf16[16,1,1]{2,1,0:T(2,128)(2,1)}), bf16[16,1,1]{2,1,0:T(2,128)(2,1)S(1)}, u32[]{:S(2)}, u32[]{:S(2)}) %all-to-all-start) | async-done | bytes 64 | tf_op jit(solution)/shard_map/all_to_all | solution.py:30
  57.2 0.4 convert_reduce_fusion
  57.6 0.1 fusion.2
  57.6 0.1 reshape.78
  57.7 41.4 %all-gather = bf16[32,1,256]{2,1,0:T(2,128)(2,1)S(1)} all-gather(bf16[1,1,256]{2,1,0:T(2,128)(2,1)S(1)} %reshape.78), channel_id=1, replica_groups=mesh['grp'=16,'blk'=32] {'blk'}, dimensions={0}, use_global_device_ids=true | all-gather | bytes 16896 | tf_op jit(solution)/shard_map/all_gather | solution.py:42
  99.1 0.1 compare_reduce_fusion
  99.2 91.5 %all-gather.3.cloned.1.call-done = bf16[8192,1024]{1,0:T(8,128)(2,1)} async-done(((bf16[256,1024]{1,0:T(8,128)(2,1)}), bf16[8192,1024]{1,0:T(8,128)(2,1)}) %all-gather.3.cloned.1.call-update) | async-done | bytes 16777232 | tf_op jit(solution)/shard_map/all_gather | solution.py:41
  190.7 11.3 %fusion.1 = f32[256]{0:T(256)S(1)} fusion(bf16[256,1024]{1,0:T(8,128)(2,1)} %bitcast.33, bf16[8192,1024]{1,0:T(8,128)(2,1)} %all-gather.3.cloned.1.call-done, s32[256]{0:T(256)S(1)} %iota_add_fusion, pred[8192]{0:T(1024)(128)(4,1)S(1)} %reshape.81), kind=kOutput, calls=%fused_computation.5 | convolution fusion | flops 4303355904 | bytes 17311744 | tf_op jit(solution)/shard_map/id,jd->ij/dot_general | solution.py:13
  202.0 0.1 max_broadcast_in_dim.15
  202.1 14.6 %all_to_all.21 = f32[16,1,16]{2,1,0:T(1,128)S(1)} all-to-all(f32[16,1,16]{2,1,0:T(1,128)S(1)} %max_broadcast_in_dim.15), channel_id=1, replica_groups=mesh['grp'=16,'blk'=32] {'grp'}, dimensions={0} | all-to-all | bytes 2048 | tf_op jit(solution)/shard_map/all_to_all | solution.py:47
  216.7 1.8 gather_fusion
  (4 shorter events, 0.0 us)
Async XLA Ops:
  6.5 184.2 %all-gather.3.cloned.1.call-start = ((), (), s32[]{:S(2)}) async-start(), calls=%async_computation.3 | async-start | bytes 17301504 | tf_op jit(solution)/shard_map/all_gather | solution.py:41
  47.2 9.9 %all-to-all-start = ((bf16[16,1,1]{2,1,0:T(2,128)(2,1)}), bf16[16,1,1]{2,1,0:T(2,128)(2,1)S(1)}, u32[]{:S(2)}, u32[]{:S(2)}) async-start(bf16[16,1,1]{2,1,0:T(2,128)(2,1)} %copy.6), calls=%async_computation | async-start | bytes 16384 | tf_op jit(solution)/shard_map/all_to_all | solution.py:30
Sparse Core Ops, SparseCore 0:
  46.0 144.6 all-gather.2
where the time goes:
time: 226 us; the launch traced here: 225 us
  waiting for transfers between devices  98.1 us (43%)
  blocking collectives  83.3 us (37%)
  between operations  13.5 us (6%)
  local copies, waits for them, and re-layouts  11.7 us (5%)
  matrix products  11.3 us (5%)
  other arithmetic  4.22 us (2%)
  starting transfers between devices  3.35 us (1%)
    all_gather x1, waiting for transfers between devices, body(): others = lax.all_gather(members, 'blk', axis=0, tiled=True)  91.5 us
    all_gather x1, blocking collectives, body(): marker = lax.all_gather(alive_marker, 'blk', axis=0, tiled=True)  41.4 us
    all_to_all x1, blocking collectives, body(): lax.all_to_all(outgoing, 'grp', split_axis=0, concat_axis=0, tiled=True)  27.3 us
    all_to_all x1, blocking collectives, body(): lax.all_to_all(top_score.reshape(clusters, slot_count), 'grp', split_axis...  14.6 us
    dot_general x1, matrix products, pair_scores(): jnp.einsum('id,jd->ij', left, right, preferred_element_type=jnp.float32)  11.3 us
    scatter x1, local copies, waits for them, and re-layouts, body(): outgoing = jnp.zeros((clusters, slot_count, feature_dim), jnp.bfloat16).a...  8.92 us
    all_to_all x1, waiting for transfers between devices, body(): lax.all_to_all(counts, 'grp', split_axis=0, concat_axis=0, tiled=True)  6.57 us
  transfers between devices with their start and end apart: 2, of which 2 were waited for; matrix products, arithmetic and copies ran while one was open for 1% of the time, Pallas kernels for 0%

commit v1 on v0

v1 whole, which is shorter than its diff:
```python
import functools

import jax
import jax.numpy as jnp
from jax import lax
from jax.experimental import pallas as pl
from jax.experimental.pallas import tpu as pltpu
from jax.sharding import PartitionSpec as P

MESH = pl.DeviceIdType.MESH
ROWS = 128
WIDTH = 1024
NY, NZ, NX = 8, 8, 4
FLOOR = -4.0

STEPS = ((0, 0, 1), (0, 0, -1), (1, 0, 0), (-1, 0, 0), (0, 1, 0), (0, -1, 0))
EDGES = (
    (0, 2), (0, 5), (0, 4), (3, 4), (1, 0), (0, 3),
    (3, 1), (2, 5), (6, 3), (8, 5), (5, 2), (5, 0),
    (4, 4), (11, 2), (13, 4), (10, 1), (9, 3), (4, 1),
    (14, 0), (7, 1), (9, 0), (17, 3), (14, 2), (16, 5),
)
PARTS = 2
LEFTS, RIGHTS = 2, 4
PHASES = (
    ((2, 4, 6, 12, 3, 5, 7, 13, 10, 14, 8, 16, 18, 11, 15, 22, 9, 17, 19, 24, 36, 23, 20, 26, 34, 40, 42), (3, 5, 6, 2, 0, 11)),
    ((28, 21, 27, 35), (17, 7, 6, 8, 5, 3)),
    ((25, 32), (1, 12, 9, 2, 17, 0)),
    ((), (11, 12, 6, 13, 7, 10)),
    ((29, 30, 44), (14, 9, 4, 6, 3, 10)),
    ((), (17, 14, 7, 2, 13, 10)),
    ((33, 38), (5, 16, 13, 12, 6, 8)),
    ((46, 48, 31, 45), (16, 15, 14, 11, 17, 0)),
    ((), (15, 22, 5, 16, 12, 7)),
    ((37, 39), (18, 8, 9, 1, 12, 14)),
    ((), (11, 18, 22, 3, 15, 1)),
    ((47, 49), (23, 19, 18, 15, 16, 7)),
    ((41, 43), (21, 5, 10, 18, 3, 16)),
    ((), (8, 13, 19, 22, 9, 23)),
    ((), (24, 20, 0, 17, 23, 9)),
    ((), (6, 11, 24, 12, 18, 8)),
    ((), (2, 15, 6, 22, 20, 9)),
    ((), (13, 15, 0, 21, 1, 6)),
    ((), (18, 4, 13, 17, 21, 11)),
    ((), (8, 20, 10, 3, 21, 11)),
)
SLOTS = len(EDGES) + 1
PART = ROWS // PARTS


def tree_offsets():
    offsets = [(0, 0, 0)]
    for parent, way in EDGES:
        offsets.append(tuple(a + b for a, b in zip(offsets[parent], STEPS[way])))
    return offsets


OFFSETS = tree_offsets()
CHILDREN = [[s + 1 for s, edge in enumerate(EDGES) if edge[0] == p] for p in range(SLOTS)]
LEFT_SLOTS = sorted({s for _, batch in PHASES for s in batch[:LEFTS]} | {0})
RIGHT_SLOTS = sorted({s for _, batch in PHASES for s in batch[LEFTS:]} | {0})


def last_use(slot):
    return max((k for k, (_, batch) in enumerate(PHASES) if slot in batch), default=0)


def first_right(slot):
    return min((k for k, (_, batch) in enumerate(PHASES) if slot in batch[LEFTS:]), default=0)


def normalize_rows(block):
    total = jnp.sum(block * block, axis=1, keepdims=True)
    return (block * lax.rsqrt(total + 1e-06)).astype(jnp.bfloat16)


def column_ids(row):
    return jnp.transpose(jnp.broadcast_to(row, (ROWS, ROWS)))


def kernel(
    rows_ref, ids_ref, out_ref,
    mine, other, ids, row_best, col_best, own_out, own_in, cross_out, cross_in,
    part_send, part_recv, ids_send, ids_recv, pair_send, pair_recv,
    own_send, own_recv, cross_send, cross_recv,
):
    grp = lax.axis_index("grp")
    blk = lax.axis_index("blk")
    y, core, z, x = grp // 2, grp % 2, blk // NX, blk % NX

    def at(offset, flip=False):
        ty = (y + offset[0] + 4 * NY) % NY
        tz = (z + offset[1] + 4 * NZ) % NZ
        tx = (x + offset[2] + 4 * NX) % NX
        return (ty * 2 + (1 - core if flip else core), tz * NX + tx)

    def negated(offset):
        return tuple(-a for a in offset)

    sibling = at((0, 0, 0), True)

    def part(slot, c):
        return pl.ds(slot * ROWS + c * PART, PART)

    def edge_copy(slot, c):
        parent, way = EDGES[slot - 1]
        return pltpu.make_async_remote_copy(
            src_ref=mine.at[part(parent, c)], dst_ref=mine.at[part(slot, c)],
            send_sem=part_send.at[slot, c], recv_sem=part_recv.at[slot, c],
            device_id=at(negated(STEPS[way])), device_id_type=MESH)

    def ids_copy(slot):
        if slot == 0:
            return pltpu.make_async_remote_copy(
                src_ref=ids.at[0, 0], dst_ref=ids.at[0, 1],
                send_sem=ids_send.at[0], recv_sem=ids_recv.at[0],
                device_id=sibling, device_id_type=MESH)
        parent, way = EDGES[slot - 1]
        return pltpu.make_async_remote_copy(
            src_ref=ids.at[parent], dst_ref=ids.at[slot],
            send_sem=ids_send.at[slot], recv_sem=ids_recv.at[slot],
            device_id=at(negated(STEPS[way])), device_id_type=MESH)

    def pair_copy(slot):
        return pltpu.make_async_remote_copy(
            src_ref=mine.at[pl.ds(slot * ROWS, ROWS)], dst_ref=other.at[pl.ds(slot * ROWS, ROWS)],
            send_sem=pair_send.at[slot], recv_sem=pair_recv.at[slot],
            device_id=sibling, device_id_type=MESH)

    def own_copy(slot):
        return pltpu.make_async_remote_copy(
            src_ref=own_out.at[slot], dst_ref=own_in.at[slot],
            send_sem=own_send.at[slot], recv_sem=own_recv.at[slot],
            device_id=at(OFFSETS[slot]), device_id_type=MESH)

    def cross_copy(slot):
        return pltpu.make_async_remote_copy(
            src_ref=cross_out.at[slot], dst_ref=cross_in.at[slot],
            send_sem=cross_send.at[slot], recv_sem=cross_recv.at[slot],
            device_id=at(OFFSETS[slot], True), device_id_type=MESH)

    barrier = pltpu.get_barrier_semaphore()
    peers = [at(step) for step in STEPS] + [sibling]
    for peer in peers:
        pl.semaphore_signal(barrier, inc=1, device_id=peer, device_id_type=MESH)

    ids[0, 0] = ids_ref[...]
    mine[0:PART, :] = normalize_rows(rows_ref[0:PART, :])
    pl.semaphore_wait(barrier, len(peers))
    for c in range(PARTS):
        if c > 0:
            mine[c * PART:(c + 1) * PART, :] = normalize_rows(rows_ref[c * PART:(c + 1) * PART, :])
        for child in CHILDREN[0]:
            edge_copy(child, c).start()
        if c == 0:
            ids_copy(0).start()
    pair_copy(0).start()
    row_best[...] = jnp.full_like(row_best, FLOOR)
    col_best[...] = jnp.full_like(col_best, FLOOR)
    ids_copy(0).wait()
    for child in CHILDREN[0]:
        ids_copy(child).start()

    def arrive(slot, c):
        edge_copy(slot, c).wait_recv()
        for child in CHILDREN[slot]:
            edge_copy(child, c).start()
        if c == 0:
            ids_copy(slot).wait_recv()
            for child in CHILDREN[slot]:
                ids_copy(child).start()
        if c == PARTS - 1 and slot in RIGHT_SLOTS:
            pair_copy(slot).start()

    def finish(slot):
        if slot in RIGHT_SLOTS:
            columns = jnp.max(col_best[slot], axis=0, keepdims=True)
            cross_out[slot] = columns[:, ROWS:]
            cross_copy(slot).start()
        if slot in LEFT_SLOTS:
            best = jnp.max(jnp.transpose(row_best[pl.ds(slot * ROWS, ROWS), :]), axis=0, keepdims=True)
            if slot in RIGHT_SLOTS:
                best = jnp.maximum(best, columns[:, :ROWS])
        else:
            best = columns[:, :ROWS]
        own_out[slot] = best
        if slot > 0:
            own_copy(slot).start()

    def own_block():
        left = mine[0:ROWS, :]
        right = jnp.concatenate([left, other[0:ROWS, :]], axis=0)
        scores = lax.dot_general(
            left, right, (((1,), (1,)), ((), ())), preferred_element_type=jnp.float32)
        down = column_ids(ids[0, 0])
        same = lax.broadcasted_iota(jnp.int32, (ROWS, ROWS), 0) == lax.broadcasted_iota(
            jnp.int32, (ROWS, ROWS), 1)
        near = jnp.where((down == ids[0, 0]) & jnp.logical_not(same), scores[:, :ROWS], FLOOR)
        far = jnp.where(down == ids[0, 1], scores[:, ROWS:], FLOOR)
        row_best[0:ROWS, :] = jnp.maximum(near, far)

    def events(phase):
        for arrival in PHASES[phase][0]:
            arrive(arrival // PARTS, arrival % PARTS)
        for slot in RIGHT_SLOTS:
            if slot > 0 and first_right(slot) == phase:
                pair_copy(slot).wait_recv()

    def batch(phase):
        code = jnp.int32(0)
        for k, (_, slots) in enumerate(PHASES):
            code = jnp.where(phase == k, sum(s << (5 * i) for i, s in enumerate(slots)), code)
        picked = [(code >> (5 * i)) & 31 for i in range(LEFTS + RIGHTS)]
        lefts, rights = picked[:LEFTS], picked[LEFTS:]

        def span(slot):
            return pl.ds(pl.multiple_of(slot * ROWS, ROWS), ROWS)

        left = jnp.concatenate([mine[span(s), :] for s in lefts], axis=0)
        right = jnp.concatenate([m[span(s), :] for s in rights for m in (mine, other)], axis=0)
        scores = lax.dot_general(
            left, right, (((1,), (1,)), ((), ())), preferred_element_type=jnp.float32)
        for i, a in enumerate(lefts):
            down = column_ids(ids[a, 0])
            best = row_best[span(a), :]
            for j, b in enumerate(rights):
                for half in range(2):
                    lane = (2 * j + half) * ROWS
                    block = scores[i * ROWS:(i + 1) * ROWS, lane:lane + ROWS]
                    block = jnp.where(down == ids[b, half], block, FLOOR)
                    best = jnp.maximum(best, block)
                    top = jnp.max(block.reshape(ROWS // 8, 8, ROWS), axis=0)
                    span_half = slice(half * ROWS, (half + 1) * ROWS)
                    col_best[b, :, span_half] = jnp.maximum(col_best[b, :, span_half], top)
            row_best[span(a), :] = best

    pair_copy(0).wait_recv()
    own_block()

    def step(phase, carry):
        for k in range(len(PHASES)):
            pl.when(phase == k)(functools.partial(events, k))
        batch(phase)
        for k in range(len(PHASES)):
            done = [s for s in range(SLOTS) if last_use(s) == k]
            if done:
                def close(done=done):
                    for slot in done:
                        finish(slot)
                pl.when(phase == k)(close)
        return carry

    lax.fori_loop(0, len(PHASES), step, 0)

    for slot in range(1, SLOTS):
        for c in range(PARTS):
            edge_copy(slot, c).wait_send()
        ids_copy(slot).wait_send()
    for slot in RIGHT_SLOTS:
        pair_copy(slot).wait_send()
    for slot in range(SLOTS):
        if slot > 0:
            own_copy(slot).wait_send()
        if slot in RIGHT_SLOTS:
            cross_copy(slot).wait_send()
    best = own_out[0]
    for slot in range(SLOTS):
        if slot > 0:
            own_copy(slot).wait_recv()
            best = jnp.maximum(best, own_in[slot])
        if slot in RIGHT_SLOTS:
            cross_copy(slot).wait_recv()
            best = jnp.maximum(best, cross_in[slot])
    out_ref[...] = best


def body(embeddings, cluster_ids, row_slots, cluster_sizes):
    dma = pltpu.SemaphoreType.DMA
    best = pl.pallas_call(
        kernel,
        out_shape=jax.ShapeDtypeStruct((1, ROWS), jnp.float32),
        in_specs=[pl.BlockSpec(memory_space=pltpu.VMEM)] * 2,
        out_specs=pl.BlockSpec(memory_space=pltpu.VMEM),
        scratch_shapes=[
            pltpu.VMEM((SLOTS * ROWS, WIDTH), jnp.bfloat16),
            pltpu.VMEM((SLOTS * ROWS, WIDTH), jnp.bfloat16),
            pltpu.VMEM((SLOTS, 2, 1, ROWS), jnp.int32),
            pltpu.VMEM((SLOTS * ROWS, ROWS), jnp.float32),
            pltpu.VMEM((SLOTS, 8, 2 * ROWS), jnp.float32),
            pltpu.VMEM((SLOTS, 1, ROWS), jnp.float32),
            pltpu.VMEM((SLOTS, 1, ROWS), jnp.float32),
            pltpu.VMEM((SLOTS, 1, ROWS), jnp.float32),
            pltpu.VMEM((SLOTS, 1, ROWS), jnp.float32),
            dma((SLOTS, PARTS)), dma((SLOTS, PARTS)), dma((SLOTS,)), dma((SLOTS,)),
            dma((SLOTS,)), dma((SLOTS,)), dma((SLOTS,)), dma((SLOTS,)),
            dma((SLOTS,)), dma((SLOTS,)),
        ],
        compiler_params=pltpu.CompilerParams(
            collective_id=1, has_side_effects=True, vmem_limit_bytes=48 * 2**20),
    )(embeddings, cluster_ids.reshape(1, ROWS))
    return best.reshape(ROWS)


def solution(mesh):
    placed = (
        P(("grp", "blk"), None),
        P(("grp", "blk")),
        P(("grp", "blk")),
        P(("grp", "blk"), None),
    )
    return jax.shard_map(
        body, mesh=mesh, in_specs=placed, out_specs=P(("grp", "blk")), check_vma=False
    )
```

time: 226 us -> 74.4 us (0.33)
  waiting for transfers between devices: 98.1 us -> 0 us
  blocking collectives: 83.3 us -> 0 us
  Pallas kernels: 0 us -> 72 us
  between operations: 13.5 us -> 0.01 us
  matrix products: 11.3 us -> 0 us
  local copies, waits for them, and re-layouts: 11.7 us -> 2.21 us
  other arithmetic: 4.22 us -> 0 us
  starting transfers between devices: 3.35 us -> 0 us
    all_gather x1 -> x0, waiting for transfers between devices: 91.5 us -> none  [body(): others = lax.all_gather(members, 'blk', axis=0, tiled=True)]
    pallas_call x0 -> x1, Pallas kernels: none -> 72 us  [body(): pl.pallas_call(kernel, out_shape=jax.ShapeDtypeStruct((1, ROWS), jnp.floa...]
    all_to_all x2 -> x0, blocking collectives: 41.9 us -> none  [the longest x1 27.3 us: body(): lax.all_to_all(outgoing, 'grp', split_axis=0, concat_axis=0, tiled=True)]
    all_gather x1 -> x0, blocking collectives: 41.4 us -> none  [body(): marker = lax.all_gather(alive_marker, 'blk', axis=0, tiled=True)]
    dot_general x1 -> x0, matrix products: 11.3 us -> none  [pair_scores(): jnp.einsum('id,jd->ij', left, right, preferred_element_type=jnp.float32)]
    scatter x1 -> x0, local copies, waits for them, and re-layouts: 8.92 us -> none  [body(): outgoing = jnp.zeros((clusters, slot_count, feature_dim), jnp.bfloat16).a...]
    all_to_all x1 -> x0, waiting for transfers between devices: 6.57 us -> none  [body(): lax.all_to_all(counts, 'grp', split_axis=0, concat_axis=0, tiled=True)]
    all_to_all x1 -> x0, starting transfers between devices: 3.34 us -> none  [body(): lax.all_to_all(counts, 'grp', split_axis=0, concat_axis=0, tiled=True)]
  transfers between devices with their start and end apart: 2 -> 0, of which waited for: 2 -> 0; matrix products, arithmetic and copies ran while one was open for 1% -> 0% of each run, Pallas kernels for 0% -> 0%
where the time goes in v1:
time: 74.4 us; the launch traced here: 74.3 us
  Pallas kernels  72 us (97%)
  local copies, waits for them, and re-layouts  2.21 us (3%)
    pallas_call x1, Pallas kernels, body(): pl.pallas_call(kernel, out_shape=jax.ShapeDtypeStruct((1, ROWS), jnp.floa...  72 us
    unnamed x5, local copies, waits for them, and re-layouts  2.21 us

profile of v1, /device:TPU:1, one launch (start us, length us, event | category | flops | bytes accessed | tf_op | source)
XLA Modules:
  0.0 74.3 jit_solution(5527819652374756155)
XLA Ops:
  0.0 0.0 copy-start.1
  0.0 0.7 copy-done.1
  0.7 0.0 copy-start
  0.7 1.0 %copy-done = f32[128,1024]{1,0:T(8,128)S(1)} copy-done((f32[128,1024]{1,0:T(8,128)S(1)}, f32[128,1024]{1,0:T(8,128)}, u32[]{:S(2)}) %copy-start) | copy-done | bytes 524312
  1.7 72.0 %shard_map.28 = f32[1,128]{1,0:T(1,128)S(1)} custom-call(f32[128,1024]{1,0:T(8,128)S(1)} %copy-done, s32[1,128]{1,0:T(1,128)S(1)} %bitcast.2), custom_call_target="tpu_custom_call" | custom-call | tf_op jit(solution)/shard_map/pallas_call | solution.py:279
  73.7 0.5 copy.4
Async XLA Ops:
  0.0 0.7 copy-start.1
  0.7 1.0 %copy-start = (f32[128,1024]{1,0:T(8,128)S(1)}, f32[128,1024]{1,0:T(8,128)}, u32[]{:S(2)}) copy-start(f32[128,1024]{1,0:T(8,128)} %rows_ref.1) | copy-start | bytes 1572868

commit v2 on v1

v2 whole, which is shorter than its diff:
```python
import functools

import jax
import jax.numpy as jnp
from jax import lax
from jax.experimental import pallas as pl
from jax.experimental.pallas import tpu as pltpu
from jax.sharding import PartitionSpec as P

MESH = pl.DeviceIdType.MESH
ROWS = 128
WIDTH = 1024
NY, NZ, NX = 8, 8, 4
FLOOR = -4.0

STEPS = ((0, 0, 1), (0, 0, -1), (1, 0, 0), (-1, 0, 0), (0, 1, 0), (0, -1, 0))
EDGES = (
    (0, 3), (1, 1), (0, 2), (0, 5), (4, 0), (5, 5),
    (0, 4), (7, 4), (6, 5), (3, 2), (10, 2), (1, 3),
    (11, 0), (12, 1), (2, 1), (14, 3), (9, 5), (8, 4),
    (16, 3), (9, 0), (7, 0), (20, 4), (11, 2), (17, 1),
)
PARTS = 4
FIRST = (15, 5, 35, 20, 16, 6, 36, 21, 17, 7, 37, 22)
PHASES = (
    ((10, 105, 25, 18, 8, 38, 23, 11, 26, 50, 60, 40, 75, 12, 27, 51, 61, 41, 30, 19, 9, 24, 39, 13, 28, 52, 62, 42, 31, 70, 106), (1, 0)),
    ((53, 63, 43), (3, 1)),
    ((32,), (4, 0, 1, 3)),
    ((107, 71, 55, 90, 45), (7, 4)),
    ((14, 29, 33, 72, 108, 56, 91, 80, 54, 64), (2, 1, 3, 4, 7)),
    ((73, 57, 92, 46, 44), (5, 0, 2, 3, 7)),
    ((100, 81, 47, 76, 65, 58, 93, 95, 34, 109, 82, 48, 77, 66, 115, 74, 110), (6, 1, 2, 3, 7)),
    ((101, 78, 116, 83, 85), (8, 1, 2, 3, 4, 6)),
    ((), (10, 2, 5, 6, 7, 8)),
    ((102, 117, 96, 86, 59, 94), (12, 7, 10, 2, 5, 6, 8)),
    ((49,), (14, 10, 5, 6, 7, 8)),
    ((103, 118, 97, 87), (21, 3, 2, 4, 0, 10, 14)),
    ((120, 84, 79, 111, 98), (9, 1, 2, 3, 10, 12, 14, 21)),
    ((67, 88), (11, 4, 5, 6, 7, 8, 9, 14, 21)),
    ((68, 121, 112), (16, 7, 5, 6, 8, 9, 11, 21)),
    ((122,), (18, 1, 2, 3, 10, 11, 12, 14, 16)),
    ((113, 104, 119), (15, 11, 10, 0, 1, 3, 6, 8, 18)),
    ((123, 89, 99), (20, 2, 0, 7, 10, 11, 14, 16)),
    ((69, 114), (17, 3, 10, 11, 12, 14, 16)),
    ((), (19, 4, 5, 6, 7, 8, 9, 17, 18)),
    ((124,), (22, 4, 10, 11, 14, 16)),
    ((), (23, 1, 7, 6, 8, 9, 17, 18)),
    ((), (13, 10, 6, 7, 8, 9, 17, 18)),
    ((), (24, 5, 2, 15, 22, 1, 10, 13, 23)),
)
SLOTS = len(EDGES) + 1
PART = ROWS // PARTS


def tree_offsets():
    offsets = [(0, 0, 0)]
    for parent, way in EDGES:
        offsets.append(tuple(a + b for a, b in zip(offsets[parent], STEPS[way])))
    return offsets


OFFSETS = tree_offsets()
CHILDREN = [[s + 1 for s, edge in enumerate(EDGES) if edge[0] == p] for p in range(SLOTS)]
ORDER = [slots[0] for _, slots in PHASES]
SIZES = (4, 6, 8)


def last_use(slot):
    return max((k for k, (_, slots) in enumerate(PHASES) if slot in slots), default=0)


def size_of(slots):
    return min(size for size in SIZES if size >= len(slots) - 1)


def padded(slots):
    return slots + slots[-1:] * (SIZES[-1] + 1 - len(slots))


def normalize_rows(block):
    total = jnp.sum(block * block, axis=1, keepdims=True)
    return (block * lax.rsqrt(total + 1e-06)).astype(jnp.bfloat16)


def column_ids(row):
    return jnp.transpose(jnp.broadcast_to(row, (ROWS, ROWS)))


def kernel(
    rows_hbm, ids_hbm, out_ref,
    rows_ref, mine, other, ids, down_ids, row_best, col_best, own_out, own_in, cross_out, cross_in,
    part_send, part_recv, ids_send, ids_recv, pair_send, pair_recv,
    own_send, own_recv, cross_send, cross_recv, load_sem,
):
    grp = lax.axis_index("grp")
    blk = lax.axis_index("blk")
    y, core, z, x = grp // 2, grp % 2, blk // NX, blk % NX

    def at(offset, flip=False):
        ty = lax.rem(y + offset[0] % NY, NY)
        tz = lax.rem(z + offset[1] % NZ, NZ)
        tx = lax.rem(x + offset[2] % NX, NX)
        return (ty * 2 + (1 - core if flip else core), tz * NX + tx)

    def negated(offset):
        return tuple(-a for a in offset)

    sibling = at((0, 0, 0), True)
    behind = [at(negated(step)) for step in STEPS]

    def part(slot, c):
        return pl.ds(slot * ROWS + c * PART, PART)

    def edge_copy(slot, c):
        parent, way = EDGES[slot - 1]
        return pltpu.make_async_remote_copy(
            src_ref=mine.at[part(parent, c)], dst_ref=mine.at[part(slot, c)],
            send_sem=part_send.at[0], recv_sem=part_recv.at[slot, c],
            device_id=behind[way], device_id_type=MESH)

    def ids_copy(slot):
        if slot == 0:
            return pltpu.make_async_remote_copy(
                src_ref=ids.at[0, 0], dst_ref=ids.at[0, 1],
                send_sem=ids_send.at[0], recv_sem=ids_recv.at[0],
                device_id=sibling, device_id_type=MESH)
        parent, way = EDGES[slot - 1]
        return pltpu.make_async_remote_copy(
            src_ref=ids.at[parent], dst_ref=ids.at[slot],
            send_sem=ids_send.at[1], recv_sem=ids_recv.at[slot],
            device_id=behind[way], device_id_type=MESH)

    def pair_copy(slot):
        return pltpu.make_async_remote_copy(
            src_ref=mine.at[pl.ds(slot * ROWS, ROWS)], dst_ref=other.at[pl.ds(slot * ROWS, ROWS)],
            send_sem=pair_send.at[0], recv_sem=pair_recv.at[slot],
            device_id=sibling, device_id_type=MESH)

    def own_copy(slot):
        return pltpu.make_async_remote_copy(
            src_ref=own_out.at[slot], dst_ref=own_in.at[slot],
            send_sem=own_send.at[0], recv_sem=own_recv.at[0],
            device_id=at(OFFSETS[slot]), device_id_type=MESH)

    def cross_copy(slot):
        return pltpu.make_async_remote_copy(
            src_ref=cross_out.at[slot], dst_ref=cross_in.at[slot],
            send_sem=cross_send.at[0], recv_sem=cross_recv.at[0],
            device_id=at(OFFSETS[slot], True), device_id_type=MESH)

    barrier = pltpu.get_barrier_semaphore()
    peers = behind + [sibling]
    for peer in peers:
        pl.semaphore_signal(barrier, inc=1, device_id=peer, device_id_type=MESH)

    loads = [
        pltpu.make_async_copy(
            rows_hbm.at[pl.ds(c * PART, PART)], rows_ref.at[pl.ds(c * PART, PART)], load_sem.at[c])
        for c in range(PARTS)]
    loads.append(pltpu.make_async_copy(ids_hbm, ids.at[0, 0], load_sem.at[PARTS]))
    for load in loads:
        load.start()

    def normalize_part(c):
        loads[c].wait()
        mine[c * PART:(c + 1) * PART, :] = normalize_rows(rows_ref[c * PART:(c + 1) * PART, :])

    normalize_part(0)
    loads[PARTS].wait()
    pl.semaphore_wait(barrier, len(peers))
    ids_copy(0).start()
    taken = set()

    def take(slot, c):
        if slot > 0 and (slot, c) not in taken:
            taken.add((slot, c))
            edge_copy(slot, c).wait_recv()

    def take_ids(slot):
        if (slot, PARTS) not in taken:
            taken.add((slot, PARTS))
            if slot == 0:
                ids_copy(0).wait()
            else:
                ids_copy(slot).wait_recv()

    def take_block(slot):
        for c in range(PARTS):
            take(slot, c)
        take_ids(slot)

    def take_pair(slot):
        if (slot, PARTS + 1) not in taken:
            taken.add((slot, PARTS + 1))
            pair_copy(slot).wait_recv()

    def act(action):
        slot, c = action // (PARTS + 1), action % (PARTS + 1)
        if c == PARTS:
            for part_ in range(PARTS):
                take(slot, part_)
            pair_copy(slot).start()
            return
        parent = EDGES[slot - 1][0]
        take(parent, c)
        if c == PARTS - 1:
            take_ids(parent)
            ids_copy(slot).start()
        edge_copy(slot, c).start()

    def finish(slot):
        best = jnp.max(jnp.transpose(row_best[span(slot), :]), axis=0, keepdims=True)
        if slot > 0:
            best = jnp.maximum(best, col_best[slot])
        own_out[slot] = best
        if slot > 0:
            own_copy(slot).start()

    def span(slot):
        if isinstance(slot, int):
            return pl.ds(slot * ROWS, ROWS)
        return pl.ds(pl.multiple_of(slot * ROWS, ROWS), ROWS)

    def own_block():
        left = mine[0:ROWS, :]
        right = jnp.concatenate([left, other[0:ROWS, :]], axis=0)
        scores = lax.dot_general(
            left, right, (((1,), (1,)), ((), ())), preferred_element_type=jnp.float32)
        down = column_ids(ids[0, 0])
        down_ids[0:ROWS, :] = down
        same = lax.broadcasted_iota(jnp.int32, (ROWS, ROWS), 0) == lax.broadcasted_iota(
            jnp.int32, (ROWS, ROWS), 1)
        near = jnp.where((down == ids[0, 0]) & jnp.logical_not(same), scores[:, :ROWS], FLOOR)
        far = jnp.where(down == ids[0, 1], scores[:, ROWS:], FLOOR)
        row_best[0:ROWS, :] = jnp.maximum(near, far)

    def events(phase):
        if phase > 0:
            cross_copy(ORDER[phase - 1]).start()
            for slot in range(SLOTS):
                if last_use(slot) == phase - 1:
                    finish(slot)
        if phase < len(PHASES):
            actions, slots = PHASES[phase]
            for action in actions:
                act(action)
            take_block(slots[0])
            take_pair(slots[0])

    def lookup(phase, values):
        found = jnp.int32(values[0])
        for k, value in enumerate(values[1:], 1):
            found = jnp.where(phase == k, value, found)
        return found

    def packed(phase, first, count):
        code = lookup(phase, [
            sum(s << (5 * i) for i, s in enumerate(padded(slots)[first:first + count]))
            for _, slots in PHASES])
        return [(code >> (5 * i)) & 31 for i in range(count)]

    def products(new, partners):
        left = jnp.concatenate([mine[span(p), :] for p in partners], axis=0)
        right = jnp.concatenate([mine[span(new), :], other[span(new), :]], axis=0)
        scores = lax.dot_general(
            left, right, (((1,), (1,)), ((), ())), preferred_element_type=jnp.float32)
        down_ids[span(new), :] = column_ids(ids[new, 0])
        top = [jnp.full((8, ROWS), FLOOR, jnp.float32)] * 2
        for i, p in enumerate(partners):
            down = down_ids[span(p), :]
            best = row_best[span(p), :]
            for half in range(2):
                block = scores[i * ROWS:(i + 1) * ROWS, half * ROWS:(half + 1) * ROWS]
                block = jnp.where(down == ids[new, half], block, FLOOR)
                best = jnp.maximum(best, block)
                top[half] = jnp.maximum(
                    top[half], jnp.max(block.reshape(ROWS // 8, 8, ROWS), axis=0))
            row_best[span(p), :] = best
        col_best[new] = jnp.max(top[0], axis=0, keepdims=True)
        cross_out[new] = jnp.max(top[1], axis=0, keepdims=True)

    def batch(phase):
        new, *partners = packed(phase, 0, 5) + packed(phase, 5, 4)
        size = lookup(phase, [size_of(slots) for _, slots in PHASES])
        for count in SIZES:
            if any(size_of(slots) == count for _, slots in PHASES):
                pl.when(size == count)(lambda count=count: products(new, partners[:count]))

    def dispatch(phase, low, high):
        if high - low == 1:
            events(low)
            return
        middle = (low + high) // 2
        pl.when(phase < middle)(lambda: dispatch(phase, low, middle))
        pl.when(phase >= middle)(lambda: dispatch(phase, middle, high))

    for c in range(PARTS):
        if c > 0:
            normalize_part(c)
        for action in FIRST:
            if action % (PARTS + 1) == c:
                act(action)
    act(PARTS)
    row_best[...] = jnp.full_like(row_best, FLOOR)
    take_pair(0)
    take_ids(0)
    own_block()

    def step(phase, carry):
        dispatch(phase, 0, len(PHASES))
        batch(phase)
        return carry

    lax.fori_loop(0, len(PHASES), step, 0)
    events(len(PHASES))

    def whole(ref, send, recv, first, count):
        rows = ref.at[pl.ds(first, count)]
        return pltpu.make_async_remote_copy(
            src_ref=rows, dst_ref=rows, send_sem=send.at[0], recv_sem=recv.at[0],
            device_id=sibling, device_id_type=MESH)

    whole(mine, part_send, part_send, 0, (SLOTS - 1) * ROWS).wait_send()
    whole(mine, pair_send, pair_send, 0, SLOTS * ROWS).wait_send()
    whole(ids, ids_send.at[pl.ds(1, 1)], ids_send.at[pl.ds(1, 1)], 0, SLOTS - 1).wait_send()
    own = whole(own_in, own_send, own_recv, 1, SLOTS - 1)
    cross = whole(cross_in, cross_send, cross_recv, 1, SLOTS - 1)
    own.wait_send()
    cross.wait_send()
    cross.wait_recv()
    own.wait_recv()
    best = own_out[0]
    for slot in range(1, SLOTS):
        best = jnp.maximum(best, jnp.maximum(own_in[slot], cross_in[slot]))
    out_ref[...] = best


def body(embeddings, cluster_ids, row_slots, cluster_sizes):
    dma = pltpu.SemaphoreType.DMA
    best = pl.pallas_call(
        kernel,
        out_shape=jax.ShapeDtypeStruct((1, ROWS), jnp.float32),
        in_specs=[pl.BlockSpec(memory_space=pl.ANY)] * 2,
        out_specs=pl.BlockSpec(memory_space=pltpu.VMEM),
        scratch_shapes=[
            pltpu.VMEM((ROWS, WIDTH), jnp.float32),
            pltpu.VMEM((SLOTS * ROWS, WIDTH), jnp.bfloat16),
            pltpu.VMEM((SLOTS * ROWS, WIDTH), jnp.bfloat16),
            pltpu.VMEM((SLOTS, 2, 1, ROWS), jnp.int32),
            pltpu.VMEM((SLOTS * ROWS, ROWS), jnp.int32),
            pltpu.VMEM((SLOTS * ROWS, ROWS), jnp.float32),
            pltpu.VMEM((SLOTS, 1, ROWS), jnp.float32),
            pltpu.VMEM((SLOTS, 1, ROWS), jnp.float32),
            pltpu.VMEM((SLOTS, 1, ROWS), jnp.float32),
            pltpu.VMEM((SLOTS, 1, ROWS), jnp.float32),
            pltpu.VMEM((SLOTS, 1, ROWS), jnp.float32),
            dma((1,)), dma((SLOTS, PARTS)), dma((2,)), dma((SLOTS,)),
            dma((1,)), dma((SLOTS,)), dma((1,)), dma((1,)),
            dma((1,)), dma((1,)), dma((PARTS + 1,)),
        ],
        compiler_params=pltpu.CompilerParams(
            collective_id=1, has_side_effects=True, vmem_limit_bytes=63 * 2**20),
    )(embeddings, cluster_ids.reshape(1, ROWS))
    return best.reshape(ROWS)


def solution(mesh):
    placed = (
        P(("grp", "blk"), None),
        P(("grp", "blk")),
        P(("grp", "blk")),
        P(("grp", "blk"), None),
    )
    return jax.shard_map(
        body, mesh=mesh, in_specs=placed, out_specs=P(("grp", "blk")), check_vma=False
    )
```

time: 74.4 us -> 62.1 us (0.83)
  Pallas kernels: 72 us -> 60.8 us
  local copies, waits for them, and re-layouts: 2.21 us -> 1.1 us
    pallas_call x1, Pallas kernels: 72 us -> 60.8 us  [body(): pl.pallas_call(kernel, out_shape=jax.ShapeDtypeStruct((1, ROWS), jnp.floa...]
    unnamed x5 -> x3, local copies, waits for them, and re-layouts: 2.21 us -> 1.1 us
where the time goes in v2:
time: 62.1 us; the launch traced here: 61.9 us
  Pallas kernels  60.8 us (98%)
  local copies, waits for them, and re-layouts  1.1 us (2%)
    pallas_call x1, Pallas kernels, body(): pl.pallas_call(kernel, out_shape=jax.ShapeDtypeStruct((1, ROWS), jnp.floa...  60.8 us

profile of v2, /device:TPU:1, one launch (start us, length us, event | category | flops | bytes accessed | tf_op | source)
XLA Modules:
  0.0 61.9 jit_solution(12774030077099733576)
XLA Ops:
  0.0 60.8 %shard_map.28 = f32[1,128]{1,0:T(1,128)} custom-call(f32[128,1024]{1,0:T(8,128)} %rows_hbm.1, s32[1,128]{1,0:T(1,128)} %bitcast.2), custom_call_target="tpu_custom_call" | custom-call | tf_op jit(solution)/shard_map/pallas_call | solution.py:340
  60.8 0.0 copy-start
  60.8 0.6 copy-done
  61.4 0.5 copy.4
Async XLA Ops:
  60.8 0.6 copy-start

commit v3 on v2

--- a/solution.py
+++ b/solution.py
@@ -15,38 +15,31 @@
 
 STEPS = ((0, 0, 1), (0, 0, -1), (1, 0, 0), (-1, 0, 0), (0, 1, 0), (0, -1, 0))
 EDGES = (
-    (0, 3), (1, 1), (0, 2), (0, 5), (4, 0), (5, 5),
-    (0, 4), (7, 4), (6, 5), (3, 2), (10, 2), (1, 3),
-    (11, 0), (12, 1), (2, 1), (14, 3), (9, 5), (8, 4),
-    (16, 3), (9, 0), (7, 0), (20, 4), (11, 2), (17, 1),
+    (0, 3), (1, 3), (2, 3), (3, 0), (0, 1), (0, 2),
+    (6, 2), (3, 3), (5, 5), (0, 4), (10, 4), (9, 5),
+    (6, 0), (11, 4), (13, 0), (11, 1), (12, 5), (7, 2),
+    (17, 1), (13, 2), (14, 4), (8, 0), (9, 1), (17, 5),
 )
 PARTS = 4
-FIRST = (15, 5, 35, 20, 16, 6, 36, 21, 17, 7, 37, 22)
+FIRST = (25, 30, 5, 50, 26, 31, 6, 51, 27, 32, 7, 52, 28, 33, 8, 53)
 PHASES = (
-    ((10, 105, 25, 18, 8, 38, 23, 11, 26, 50, 60, 40, 75, 12, 27, 51, 61, 41, 30, 19, 9, 24, 39, 13, 28, 52, 62, 42, 31, 70, 106), (1, 0)),
-    ((53, 63, 43), (3, 1)),
-    ((32,), (4, 0, 1, 3)),
-    ((107, 71, 55, 90, 45), (7, 4)),
-    ((14, 29, 33, 72, 108, 56, 91, 80, 54, 64), (2, 1, 3, 4, 7)),
-    ((73, 57, 92, 46, 44), (5, 0, 2, 3, 7)),
-    ((100, 81, 47, 76, 65, 58, 93, 95, 34, 109, 82, 48, 77, 66, 115, 74, 110), (6, 1, 2, 3, 7)),
-    ((101, 78, 116, 83, 85), (8, 1, 2, 3, 4, 6)),
-    ((), (10, 2, 5, 6, 7, 8)),
-    ((102, 117, 96, 86, 59, 94), (12, 7, 10, 2, 5, 6, 8)),
-    ((49,), (14, 10, 5, 6, 7, 8)),
-    ((103, 118, 97, 87), (21, 3, 2, 4, 0, 10, 14)),
-    ((120, 84, 79, 111, 98), (9, 1, 2, 3, 10, 12, 14, 21)),
-    ((67, 88), (11, 4, 5, 6, 7, 8, 9, 14, 21)),
-    ((68, 121, 112), (16, 7, 5, 6, 8, 9, 11, 21)),
-    ((122,), (18, 1, 2, 3, 10, 11, 12, 14, 16)),
-    ((113, 104, 119), (15, 11, 10, 0, 1, 3, 6, 8, 18)),
-    ((123, 89, 99), (20, 2, 0, 7, 10, 11, 14, 16)),
-    ((69, 114), (17, 3, 10, 11, 12, 14, 16)),
-    ((), (19, 4, 5, 6, 7, 8, 9, 17, 18)),
-    ((124,), (22, 4, 10, 11, 14, 16)),
-    ((), (23, 1, 7, 6, 8, 9, 17, 18)),
-    ((), (13, 10, 6, 7, 8, 9, 17, 18)),
-    ((), (24, 5, 2, 15, 22, 1, 10, 13, 23)),
+    ((45, 65, 35, 10, 55, 46, 66, 36, 11, 56, 47, 67, 115, 60, 75, 37, 12, 57, 29, 34, 9, 54, 48, 68, 116, 38, 13, 58, 80, 61, 76), (1, 0)),
+    ((117,), (5, 0)),
+    ((90, 15, 70), (6, 1, 5)),
+    ((77, 81, 62), (10, 1, 6)),
+    ((91, 16, 71, 85, 49, 69, 78, 118, 92, 17, 72, 39, 14, 59, 63, 82), (9, 1, 6)),
+    ((93, 18, 73, 20, 86), (2, 6, 5, 9, 10)),
+    ((83,), (11, 5, 0, 1, 2, 6)),
+    ((21, 100, 40, 105, 87, 79, 95, 119, 101, 41, 106, 22, 120, 64), (23, 6, 11, 10, 2)),
+    ((), (13, 10, 23)),
+    ((23, 96, 102, 42, 107, 88, 19, 74, 94), (12, 9, 1, 2, 6, 11, 13), (7, 2, 5, 9, 10, 11, 12, 23)),
+    ((110, 97, 103, 43, 108, 121, 84), (3, 2, 5, 13, 9, 10, 11, 12)),
+    ((111,), (14, 5, 1, 2, 3, 6, 7, 13, 23), (15, 2, 0, 3, 6, 10, 11, 12, 14)),
+    ((112, 122, 98, 24, 89), (16, 11, 3, 6, 9, 2, 10, 12), (18, 15, 9, 10, 11, 12, 14, 16, 23)),
+    ((113, 123, 44, 104, 109), (17, 14, 1, 2, 3, 6, 7, 15, 18), (4, 7, 9, 10, 12, 14, 16, 17, 23)),
+    ((99,), (8, 9, 10, 11, 12, 14, 16, 17, 23), (20, 15, 11, 17, 10, 12, 14, 16, 23)),
+    ((114, 124), (21, 6, 2, 3, 4, 8, 13, 15, 20), (19, 12, 6, 2, 4, 8, 18, 20, 21)),
+    ((), (24, 23, 15, 2, 4, 18, 20), (22, 23, 16, 19, 21, 24)),
 )
 SLOTS = len(EDGES) + 1
 PART = ROWS // PARTS
@@ -61,20 +54,24 @@
 
 OFFSETS = tree_offsets()
 CHILDREN = [[s + 1 for s, edge in enumerate(EDGES) if edge[0] == p] for p in range(SLOTS)]
-ORDER = [slots[0] for _, slots in PHASES]
-SIZES = (4, 6, 8)
+SINGLE, DOUBLE = (4, 6, 8), (6, 8)
+WIDEST = 8
 
 
 def last_use(slot):
-    return max((k for k, (_, slots) in enumerate(PHASES) if slot in slots), default=0)
-
-
-def size_of(slots):
-    return min(size for size in SIZES if size >= len(slots) - 1)
-
-
-def padded(slots):
-    return slots + slots[-1:] * (SIZES[-1] + 1 - len(slots))
+    return max((k for k, (_, *groups) in enumerate(PHASES) if any(slot in g for g in groups)), default=0)
+
+
+def shape_of(groups):
+    sizes = SINGLE if len(groups) == 1 else DOUBLE
+    return len(groups), min(s for s in sizes if s >= max(len(g) for g in groups) - 1)
+
+
+SHAPES = sorted({shape_of(groups) for _, *groups in PHASES})
+
+
+def padded(group):
+    return group + group[-1:] * (WIDEST + 1 - len(group))
 
 
 def normalize_rows(block):
@@ -236,16 +233,18 @@
 
     def events(phase):
         if phase > 0:
-            cross_copy(ORDER[phase - 1]).start()
+            for group in PHASES[phase - 1][1:]:
+                cross_copy(group[0]).start()
             for slot in range(SLOTS):
                 if last_use(slot) == phase - 1:
                     finish(slot)
         if phase < len(PHASES):
-            actions, slots = PHASES[phase]
+            actions, *groups = PHASES[phase]
             for action in actions:
                 act(action)
-            take_block(slots[0])
-            take_pair(slots[0])
+            for group in groups:
+                take_block(group[0])
+                take_pair(group[0])
 
     def lookup(phase, values):
         found = jnp.int32(values[0])
@@ -253,10 +252,10 @@
             found = jnp.where(phase == k, value, found)
         return found
 
-    def packed(phase, first, count):
+    def packed(phase, member, first, count):
         code = lookup(phase, [
-            sum(s << (5 * i) for i, s in enumerate(padded(slots)[first:first + count]))
-            for _, slots in PHASES])
+            sum(s << (5 * i) for i, s in enumerate(padded(groups[min(member, len(groups) - 1)])[first:first + count]))
+            for _, *groups in PHASES])
         return [(code >> (5 * i)) & 31 for i in range(count)]
 
     def products(new, partners):
@@ -280,11 +279,13 @@
         cross_out[new] = jnp.max(top[1], axis=0, keepdims=True)
 
     def batch(phase):
-        new, *partners = packed(phase, 0, 5) + packed(phase, 5, 4)
-        size = lookup(phase, [size_of(slots) for _, slots in PHASES])
-        for count in SIZES:
-            if any(size_of(slots) == count for _, slots in PHASES):
-                pl.when(size == count)(lambda count=count: products(new, partners[:count]))
+        shape = lookup(phase, [SHAPES.index(shape_of(groups)) for _, *groups in PHASES])
+        members = [packed(phase, m, 0, 5) + packed(phase, m, 5, 4) for m in range(2)]
+        for index, (count, size) in enumerate(SHAPES):
+            def run(count=count, size=size):
+                for new, *partners in members[:count]:
+                    products(new, partners[:size])
+            pl.when(shape == index)(run)
 
     def dispatch(phase, low, high):
         if high - low == 1:
@@ -359,7 +360,7 @@
             dma((1,)), dma((1,)), dma((PARTS + 1,)),
         ],
         compiler_params=pltpu.CompilerParams(
-            collective_id=1, has_side_effects=True, vmem_limit_bytes=63 * 2**20),
+            collective_id=1, has_side_effects=True, vmem_limit_bytes=64 * 2**20 - 2**18),
     )(embeddings, cluster_ids.reshape(1, ROWS))
     return best.reshape(ROWS)
 

time: 62.1 us -> 58.4 us (0.940)
  Pallas kernels: 60.8 us -> 57.2 us
    pallas_call x1, Pallas kernels: 60.8 us -> 57.2 us  [body(): pl.pallas_call(kernel, out_shape=jax.ShapeDtypeStruct((1, ROWS), jnp.floa...]
where the time goes in v3:
time: 58.4 us; the launch traced here: 58.3 us
  Pallas kernels  57.2 us (98%)
  local copies, waits for them, and re-layouts  1.1 us (2%)
    pallas_call x1, Pallas kernels, body(): pl.pallas_call(kernel, out_shape=jax.ShapeDtypeStruct((1, ROWS), jnp.floa...  57.2 us

profile of v3, /device:TPU:1, one launch (start us, length us, event | category | flops | bytes accessed | tf_op | source)
XLA Modules:
  0.0 58.3 jit_solution(12206003851632462851)
XLA Ops:
  0.0 57.2 %shard_map.28 = f32[1,128]{1,0:T(1,128)} custom-call(f32[128,1024]{1,0:T(8,128)} %rows_hbm.1, s32[1,128]{1,0:T(1,128)} %bitcast.2), custom_call_target="tpu_custom_call" | custom-call | tf_op jit(solution)/shard_map/pallas_call | solution.py:341
  57.2 0.0 copy-start
  57.2 0.6 %copy-done = f32[1,128]{1,0:T(1,128)S(1)} copy-done((f32[1,128]{1,0:T(1,128)S(1)}, f32[1,128]{1,0:T(1,128)}, u32[]{:S(2)}) %copy-start) | copy-done | bytes 536
  57.8 0.5 copy.4
Async XLA Ops:
  57.2 0.6 %copy-start = (f32[1,128]{1,0:T(1,128)S(1)}, f32[1,128]{1,0:T(1,128)}, u32[]{:S(2)}) copy-start(f32[1,128]{1,0:T(1,128)} %shard_map.28) | copy-start | bytes 1540

commit v4 on v3

--- a/solution.py
+++ b/solution.py
@@ -25,21 +25,21 @@
 PHASES = (
     ((45, 65, 35, 10, 55, 46, 66, 36, 11, 56, 47, 67, 115, 60, 75, 37, 12, 57, 29, 34, 9, 54, 48, 68, 116, 38, 13, 58, 80, 61, 76), (1, 0)),
     ((117,), (5, 0)),
-    ((90, 15, 70), (6, 1, 5)),
-    ((77, 81, 62), (10, 1, 6)),
-    ((91, 16, 71, 85, 49, 69, 78, 118, 92, 17, 72, 39, 14, 59, 63, 82), (9, 1, 6)),
-    ((93, 18, 73, 20, 86), (2, 6, 5, 9, 10)),
-    ((83,), (11, 5, 0, 1, 2, 6)),
-    ((21, 100, 40, 105, 87, 79, 95, 119, 101, 41, 106, 22, 120, 64), (23, 6, 11, 10, 2)),
-    ((), (13, 10, 23)),
-    ((23, 96, 102, 42, 107, 88, 19, 74, 94), (12, 9, 1, 2, 6, 11, 13), (7, 2, 5, 9, 10, 11, 12, 23)),
-    ((110, 97, 103, 43, 108, 121, 84), (3, 2, 5, 13, 9, 10, 11, 12)),
-    ((111,), (14, 5, 1, 2, 3, 6, 7, 13, 23), (15, 2, 0, 3, 6, 10, 11, 12, 14)),
-    ((112, 122, 98, 24, 89), (16, 11, 3, 6, 9, 2, 10, 12), (18, 15, 9, 10, 11, 12, 14, 16, 23)),
-    ((113, 123, 44, 104, 109), (17, 14, 1, 2, 3, 6, 7, 15, 18), (4, 7, 9, 10, 12, 14, 16, 17, 23)),
-    ((99,), (8, 9, 10, 11, 12, 14, 16, 17, 23), (20, 15, 11, 17, 10, 12, 14, 16, 23)),
-    ((114, 124), (21, 6, 2, 3, 4, 8, 13, 15, 20), (19, 12, 6, 2, 4, 8, 18, 20, 21)),
-    ((), (24, 23, 15, 2, 4, 18, 20), (22, 23, 16, 19, 21, 24)),
+    ((90, 15, 70), (6, 1)),
+    ((77, 81, 62), (10, 5, 1, 6)),
+    ((91, 16, 71, 85, 49, 69, 78, 118, 92, 17, 72, 39, 14, 59, 63, 82, 93, 18, 73, 20, 86), (2, 6, 10)),
+    ((83,), (9, 1, 2, 6, 10), (13, 0, 1, 5, 9, 10)),
+    ((21, 95, 100, 40, 105, 87, 79, 119), (7, 9, 10)),
+    ((), (11, 10, 0, 1, 2, 6, 7, 9)),
+    ((22, 101, 41, 106, 88, 64), (23, 13, 1, 11, 7, 0, 2)),
+    ((23, 102, 42, 107, 19, 74, 94, 96, 120, 84, 103, 43, 108, 110, 121, 97), (3, 5, 6, 13, 9, 10, 11), (12, 1, 2, 3, 6, 7, 11, 13, 23)),
+    ((111, 98, 122, 89), (16, 6, 9, 13, 1, 0, 2), (18, 9, 10, 11, 12, 16, 23)),
+    ((112, 24), (14, 1, 2, 3, 6, 7, 13, 18, 23)),
+    ((123, 104, 113, 44, 109), (4, 7, 9, 10, 11, 12, 14, 16, 23), (17, 11, 1, 2, 3, 6, 7, 13, 18)),
+    ((99,), (8, 9, 10, 11, 12, 14, 16, 17, 23), (20, 7, 11, 17, 10, 12, 14, 16, 23)),
+    ((114, 124), (21, 0, 1, 2, 18, 4, 8, 13, 20), (19, 3, 13, 2, 4, 8, 14, 18, 20)),
+    ((), (22, 2, 3, 23, 16, 14, 21), (24, 1, 2, 4, 18, 20, 22)),
+    ((), (15, 2, 1, 3, 6, 14, 21)),
 )
 SLOTS = len(EDGES) + 1
 PART = ROWS // PARTS
@@ -60,6 +60,10 @@
 
 def last_use(slot):
     return max((k for k, (_, *groups) in enumerate(PHASES) if any(slot in g for g in groups)), default=0)
+
+
+def hops(slot):
+    return sum(min(a % n, n - a % n) for a, n in zip(OFFSETS[slot], (NY, NZ, NX)))
 
 
 def shape_of(groups):
@@ -235,7 +239,7 @@
         if phase > 0:
             for group in PHASES[phase - 1][1:]:
                 cross_copy(group[0]).start()
-            for slot in range(SLOTS):
+            for slot in sorted(range(SLOTS), key=hops, reverse=True):
                 if last_use(slot) == phase - 1:
                     finish(slot)
         if phase < len(PHASES):
@@ -333,14 +337,14 @@
     best = own_out[0]
     for slot in range(1, SLOTS):
         best = jnp.maximum(best, jnp.maximum(own_in[slot], cross_in[slot]))
-    out_ref[...] = best
+    out_ref[...] = best[0]
 
 
 def body(embeddings, cluster_ids, row_slots, cluster_sizes):
     dma = pltpu.SemaphoreType.DMA
     best = pl.pallas_call(
         kernel,
-        out_shape=jax.ShapeDtypeStruct((1, ROWS), jnp.float32),
+        out_shape=jax.ShapeDtypeStruct((ROWS,), jnp.float32),
         in_specs=[pl.BlockSpec(memory_space=pl.ANY)] * 2,
         out_specs=pl.BlockSpec(memory_space=pltpu.VMEM),
         scratch_shapes=[
@@ -362,7 +366,7 @@
         compiler_params=pltpu.CompilerParams(
             collective_id=1, has_side_effects=True, vmem_limit_bytes=64 * 2**20 - 2**18),
     )(embeddings, cluster_ids.reshape(1, ROWS))
-    return best.reshape(ROWS)
+    return best
 
 
 def solution(mesh):

time: 58.4 us -> 58.3 us (level)
    unnamed x3 -> x1, local copies, waits for them, and re-layouts: 1.1 us -> 1.19 us
where the time goes in v4:
time: 58.3 us; the launch traced here: 58.2 us
  Pallas kernels  57 us (98%)
  local copies, waits for them, and re-layouts  1.19 us (2%)
    pallas_call x1, Pallas kernels, body(): pl.pallas_call(kernel, out_shape=jax.ShapeDtypeStruct((ROWS,), jnp.float3...  57 us
    unnamed x1, local copies, waits for them, and re-layouts  1.19 us

profile of v4, /device:TPU:1, one launch (start us, length us, event | category | flops | bytes accessed | tf_op | source)
XLA Modules:
  0.0 58.2 jit_solution(8433886190453811339)
XLA Ops:
  0.0 57.0 %shard_map.28 = f32[128]{0:T(128)} custom-call(f32[128,1024]{1,0:T(8,128)} %rows_hbm.1, s32[1,128]{1,0:T(1,128)} %bitcast.1), custom_call_target="tpu_custom_call" | custom-call | tf_op jit(solution)/shard_map/pallas_call | solution.py:345
  57.0 1.2 %copy.4 = f32[128]{0:T(128)} copy(f32[128]{0:T(128)} %shard_map.28) | data formatting | bytes 1024

commit v5 on v4

--- a/solution.py
+++ b/solution.py
@@ -20,26 +20,28 @@
     (6, 0), (11, 4), (13, 0), (11, 1), (12, 5), (7, 2),
     (17, 1), (13, 2), (14, 4), (8, 0), (9, 1), (17, 5),
 )
-PARTS = 4
-FIRST = (25, 30, 5, 50, 26, 31, 6, 51, 27, 32, 7, 52, 28, 33, 8, 53)
+PARTS = 2
+FIRST = (15, 18, 3, 30, 16, 19, 4, 31)
 PHASES = (
-    ((45, 65, 35, 10, 55, 46, 66, 36, 11, 56, 47, 67, 115, 60, 75, 37, 12, 57, 29, 34, 9, 54, 48, 68, 116, 38, 13, 58, 80, 61, 76), (1, 0)),
-    ((117,), (5, 0)),
-    ((90, 15, 70), (6, 1)),
-    ((77, 81, 62), (10, 5, 1, 6)),
-    ((91, 16, 71, 85, 49, 69, 78, 118, 92, 17, 72, 39, 14, 59, 63, 82, 93, 18, 73, 20, 86), (2, 6, 10)),
-    ((83,), (9, 1, 2, 6, 10), (13, 0, 1, 5, 9, 10)),
-    ((21, 95, 100, 40, 105, 87, 79, 119), (7, 9, 10)),
-    ((), (11, 10, 0, 1, 2, 6, 7, 9)),
-    ((22, 101, 41, 106, 88, 64), (23, 13, 1, 11, 7, 0, 2)),
-    ((23, 102, 42, 107, 19, 74, 94, 96, 120, 84, 103, 43, 108, 110, 121, 97), (3, 5, 6, 13, 9, 10, 11), (12, 1, 2, 3, 6, 7, 11, 13, 23)),
-    ((111, 98, 122, 89), (16, 6, 9, 13, 1, 0, 2), (18, 9, 10, 11, 12, 16, 23)),
-    ((112, 24), (14, 1, 2, 3, 6, 7, 13, 18, 23)),
-    ((123, 104, 113, 44, 109), (4, 7, 9, 10, 11, 12, 14, 16, 23), (17, 11, 1, 2, 3, 6, 7, 13, 18)),
-    ((99,), (8, 9, 10, 11, 12, 14, 16, 17, 23), (20, 7, 11, 17, 10, 12, 14, 16, 23)),
-    ((114, 124), (21, 0, 1, 2, 18, 4, 8, 13, 20), (19, 3, 13, 2, 4, 8, 14, 18, 20)),
-    ((), (22, 2, 3, 23, 16, 14, 21), (24, 1, 2, 4, 18, 20, 22)),
-    ((), (15, 2, 1, 3, 6, 14, 21)),
+    ((27, 39, 21, 6, 33, 28, 17, 20, 40, 22, 7, 34, 5, 32, 69, 36, 45), (1, 0)),
+    ((), (5, 1)),
+    ((60,), (6, 0, 5)),
+    ((48, 9, 42), (10, 5, 6)),
+    ((37, 29, 46, 41, 61, 23, 10, 43, 8, 35, 49), (9, 1, 6)),
+    ((), (13, 6, 5, 9, 10)),
+    ((51,), (2, 5, 13, 9, 10)),
+    ((), (7, 2, 9, 10)),
+    ((12, 54, 24, 63), (11, 10, 0, 1, 2, 6, 7, 9, 13)),
+    ((70, 52, 38, 47, 55, 62, 13, 25, 64, 11, 44, 50), (12, 0, 1, 2, 6, 7, 11, 13)),
+    ((), (15, 2, 1, 6, 10, 11, 12)),
+    ((57, 72), (3, 0, 9, 10, 11, 12, 15), (14, 0, 1, 2, 3, 6, 7, 12, 13)),
+    ((66, 71), (20, 2, 0, 9, 10, 12, 14), (16, 3, 0, 2, 7, 12, 20)),
+    ((58, 73, 53, 14), (23, 15, 13, 12, 11, 14, 0, 2, 20)),
+    ((67, 26, 56, 65), (4, 0, 9, 10, 12, 14, 16, 23), (17, 1, 2, 3, 6, 7, 13, 15, 20)),
+    ((), (8, 9, 10, 11, 12, 14, 16, 17, 23), (18, 9, 10, 11, 12, 14, 16, 17, 23)),
+    ((59,), (21, 6, 7, 18, 4, 8, 13, 15, 20)),
+    ((74, 68), (19, 1, 3, 2, 4, 8, 14, 18, 20)),
+    ((), (22, 20, 23, 16, 19, 21), (24, 15, 2, 4, 18, 20, 22)),
 )
 SLOTS = len(EDGES) + 1
 PART = ROWS // PARTS

time: 58.3 us -> 58.1 us (level)
  no operation moved by 1% of the time
where the time goes in v5:
time: 58.1 us; the launch traced here: 58 us
  Pallas kernels  56.8 us (98%)
  local copies, waits for them, and re-layouts  1.19 us (2%)
    pallas_call x1, Pallas kernels, body(): pl.pallas_call(kernel, out_shape=jax.ShapeDtypeStruct((ROWS,), jnp.float3...  56.8 us
    unnamed x1, local copies, waits for them, and re-layouts  1.19 us

profile of v5, /device:TPU:1, one launch (start us, length us, event | category | flops | bytes accessed | tf_op | source)
XLA Modules:
  0.0 58.0 jit_solution(6302588704221196034)
XLA Ops:
  0.0 56.8 %shard_map.28 = f32[128]{0:T(128)} custom-call(f32[128,1024]{1,0:T(8,128)} %rows_hbm.1, s32[1,128]{1,0:T(1,128)} %bitcast.1), custom_call_target="tpu_custom_call" | custom-call | tf_op jit(solution)/shard_map/pallas_call | solution.py:347
  56.8 1.2 %copy.4 = f32[128]{0:T(128)} copy(f32[128]{0:T(128)} %shard_map.28) | data formatting | bytes 1024
